TPU v7x, 32 devices: a whole 2x2x4 slice. The times are simulated.
32 devices in a mesh: pipe: 4 (over y, core), expert: 4 (over z), tensor: 2 (over x).
Axes of the slice: x: 2, y: 2, z: 4, core: 2. Of those that a mesh axis runs over, the one named last changes fastest.
Arguments:
- sent_grad: bfloat16 [4, 512, 3584], P('pipe', 'expert', 'tensor'), may hold values from -4 to 4
- head_grad: bfloat16 [512, 3584], P('expert', 'tensor'), may hold values from -4 to 4
- probs: bfloat16 [4, 512, 8], P('pipe', 'expert'), may hold values from 0.049804688 to 1
- expert_ids: int32 [4, 512, 8], P('pipe', 'expert'), may hold values from 0 to 63, as said below
- hidden_act: bfloat16 [4, 64, 68, 1024], P('pipe', 'expert', None, 'tensor'), may hold values from -0.75 to 0.75
Outputs:
- w_down_grad: bfloat16 [4, 64, 1024, 3584], P('pipe', 'expert', 'tensor')
Inputs may be any that keep to these rules, and one draw needn't show every extreme that they name: `expert_ids`: each token names 8 different experts. In each section and each block of 128 tokens one expert is named by exactly 17 pairs, one by 17 - 2 pairs, and every other expert by 17 - 1 pairs.
All inputs are finite; a program needn't handle non-finite values.
Results may differ from a plain program's by a relative error of at most 0.0049.
Values may be sent and summed in bfloat16 or wider, within the bound.
No kernel may reach another device: no remote copies, remote signals or barrier semaphores. Data moves between devices by JAX's collectives and lax.ppermute only.
A program may use at most 192 MiB of HBM per device.

v0:
```python
import functools

import jax
import jax.numpy as jnp
from jax import lax
from jax.experimental import pallas as pl
from jax.experimental.pallas import tpu as pltpu
from jax.sharding import PartitionSpec as P

EXPERTS = 64
TOPK = 8
TOK = 128
MOST = 17
ROOM = 32
GROUPS = 2
BUFFERS = 4
CHUNKS = (768, 1024)
NOTES = 128


def passed_along(array, axis, by):
    peers = lax.axis_size(axis)
    pairs = [(i, i + by) for i in range(peers) if 0 <= i + by < peers]
    return lax.ppermute(array, axis, pairs)


def slot_ranks(pair_ids):
    onehot = (pair_ids[:, :, None] == jnp.arange(EXPERTS, dtype=jnp.int32)[None, None, :]).astype(
        jnp.int32
    )
    before = jnp.cumsum(onehot, axis=1) - onehot
    return jnp.sum(before * onehot, axis=2)


def place_rows(targets, capacity, source_rows, gate_values):
    pair_count = targets.shape[0]
    owner_pair = (
        jnp.full((capacity,), pair_count, jnp.int32)
        .at[targets]
        .set(jnp.arange(pair_count, dtype=jnp.int32), mode="drop")
    )
    filled = owner_pair < pair_count
    safe_pair = jnp.minimum(owner_pair, pair_count - 1)
    placed = jnp.where(
        filled[:, None], source_rows[safe_pair // TOPK], jnp.zeros((), source_rows.dtype)
    )
    placed_gate = jnp.where(
        filled, gate_values.reshape(-1)[safe_pair], jnp.zeros((), gate_values.dtype)
    )
    return (placed, placed_gate)


def arriving(sent_grad, head_grad):
    shifted = passed_along(sent_grad, "pipe", -1)
    is_last = lax.axis_index("pipe") == lax.axis_size("pipe") - 1
    return jnp.where(is_last, head_grad, shifted[0])


def local_by_slots(sent_grad, head_grad, probs, expert_ids, hidden_act):
    incoming = arriving(sent_grad, head_grad)
    feat_dev = incoming.shape[1]
    local_ids = expert_ids[0].reshape(1, TOK * TOPK)
    local_targets = (local_ids * MOST + slot_ranks(local_ids)).reshape(-1)
    send_rows, send_gate = place_rows(local_targets, EXPERTS * MOST, incoming, probs[0])
    recv_rows, recv_gate = (
        lax.all_to_all(
            send_rows.reshape(EXPERTS, MOST, feat_dev),
            "expert",
            split_axis=0,
            concat_axis=1,
            tiled=True,
        ),
        lax.all_to_all(
            send_gate.reshape(EXPERTS, MOST), "expert", split_axis=0, concat_axis=1, tiled=True
        ),
    )
    gate_wide = recv_gate.astype(jnp.float32)[:, :, None]
    full_rows = lax.all_gather(recv_rows, "tensor", axis=2, tiled=True)
    weighted = (full_rows.astype(jnp.float32) * gate_wide).astype(jnp.bfloat16)
    weight_grad = jnp.einsum(
        "esh,esd->ehd", hidden_act[0], weighted, preferred_element_type=jnp.float32
    ).astype(jnp.bfloat16)
    return weight_grad[None]


def join_kernel(shifted_ref, head_ref, ids_ref, probs_ref, *out_refs):
    is_last = lax.axis_index("pipe") == lax.axis_size("pipe") - 1
    rows = jnp.where(is_last, head_ref[...], shifted_ref[...])
    whole_ref, *chunk_refs = out_refs
    whole_ref[...] = rows
    offset = 0
    for span, chunk_ref in zip(CHUNKS, chunk_refs):
        chunk_ref[:, :span] = rows[:, offset : offset + span]
        offset += span
    first_ref, span = chunk_refs[0], CHUNKS[0]
    first_ref[: 2 * TOPK, span:] = jnp.concatenate(
        [ids_ref[...].astype(jnp.float32), probs_ref[...].astype(jnp.float32)], axis=0
    ).astype(jnp.bfloat16)
    first_ref[2 * TOPK :, span:] = jnp.zeros((TOK - 2 * TOPK, NOTES), jnp.bfloat16)


def place_kernel(owned, *refs):
    *blocks, place_ref = refs
    first = lax.axis_index("expert") * owned
    experts = (first + lax.broadcasted_iota(jnp.int32, (owned, TOK), 0)).astype(jnp.float32)
    earlier = (
        lax.broadcasted_iota(jnp.int32, (TOK, TOK), 0)
        < lax.broadcasted_iota(jnp.int32, (TOK, TOK), 1)
    ).astype(jnp.float32)
    ranks = lax.broadcasted_iota(jnp.int32, (ROOM, TOK), 0).astype(jnp.float32)
    for k, block in enumerate(blocks):
        meta = block[: 2 * TOPK, CHUNKS[0] :].astype(jnp.float32)
        named = jnp.zeros((owned, TOK), jnp.float32)
        gate = jnp.zeros((owned, TOK), jnp.float32)
        for c in range(TOPK):
            hit = experts == meta[c : c + 1, :]
            named = jnp.where(hit, 1.0, named)
            gate = jnp.where(hit, meta[TOPK + c : TOPK + c + 1, :], gate)
        rank = jnp.dot(named, earlier, preferred_element_type=jnp.float32)
        rank = jnp.where(named > 0.0, rank, -1.0)
        for e in range(owned):
            place_ref[k, e * ROOM : (e + 1) * ROOM, :] = jnp.where(
                ranks == rank[e : e + 1, :], gate[e : e + 1, :], 0.0
            ).astype(jnp.bfloat16)


def grad_kernel(n_expert, other, offset, feat_dev, starts, place_ref, act_ref, *refs):
    blocks = refs[:n_expert]
    out_ref, weighted_ref, done_ref, out_sem = refs[-4:]
    owned, hid, _ = act_ref.shape
    features = done_ref.shape[2]
    me = lax.axis_index("expert")
    side = lax.rem(lax.axis_index("tensor") + other, lax.axis_size("tensor"))
    column = pl.multiple_of(side * feat_dev + offset, 128)
    share = owned // GROUPS

    def leave(e):
        slot = lax.rem(e, BUFFERS)
        return pltpu.make_async_copy(
            done_ref.at[slot], out_ref.at[e, :, pl.ds(column, features)], out_sem.at[slot]
        )

    def tiles():
        for n in range(0, features, 256):
            yield n, min(n + 256, features)

    @pl.loop(0, GROUPS)
    def _(g):
        first = pl.multiple_of(g * share * ROOM, share * ROOM)
        for k in range(n_expert):
            block = lax.rem(me + n_expert - k, n_expert)
            spot = pl.ds(pl.multiple_of(block * ROOM, ROOM), ROOM)
            for low, high in tiles():
                weighted = jnp.dot(
                    place_ref[k, pl.ds(first, share * ROOM), :],
                    blocks[k][:, starts[k] + low : starts[k] + high],
                    preferred_element_type=jnp.float32,
                ).astype(jnp.bfloat16)
                for j in range(share):
                    weighted_ref[j, spot, low:high] = weighted[j * ROOM : (j + 1) * ROOM]

        @pl.loop(0, share)
        def _(j):
            e = g * share + j

            @pl.when(e >= BUFFERS)
            def _():
                leave(e - BUFFERS).wait()

            for low, high in tiles():
                done_ref[lax.rem(e, BUFFERS), :, low:high] = jnp.dot(
                    act_ref[e], weighted_ref[j, :, low:high], preferred_element_type=jnp.float32
                ).astype(jnp.bfloat16)
            leave(e).start()

    @pl.loop(owned - BUFFERS, owned)
    def _(e):
        leave(e).wait()


def local_by_tokens(sent_grad, head_grad, probs, expert_ids, hidden_act):
    n_expert = lax.axis_size("expert")
    n_tensor = lax.axis_size("tensor")
    owned, _, hid = hidden_act.shape[1:]
    feat_dev = sent_grad.shape[2]
    vmem = pl.BlockSpec(memory_space=pltpu.VMEM)
    anywhere = pl.BlockSpec(memory_space=pl.ANY)

    def small_call(kernel, shapes, operands, name):
        return pl.pallas_call(
            kernel,
            out_shape=[jax.ShapeDtypeStruct(shape, jnp.bfloat16) for shape in shapes],
            in_specs=[vmem] * len(operands),
            out_specs=[vmem] * len(shapes),
            compiler_params=pltpu.CompilerParams(vmem_limit_bytes=8 * 2**20),
            name=name,
        )(*operands)

    def turned(array, axis, by):
        peers = lax.axis_size(axis)
        return lax.ppermute(array, axis, [(i, (i + by) % peers) for i in range(peers)])

    def across(array):
        return {t: turned(array, "tensor", t) for t in range(1, n_tensor)}

    act = hidden_act[0].reshape(owned, n_expert, MOST, hid)
    act = jnp.pad(act, ((0, 0), (0, 0), (0, ROOM - MOST), (0, 0)))
    act = jnp.swapaxes(act.reshape(owned, n_expert * ROOM, hid), 1, 2)

    def grad_into(out, blocks, starts, other, chunk):
        span, offset = CHUNKS[chunk], sum(CHUNKS[:chunk])
        operands = [place, act, *blocks]
        in_specs = [vmem] * len(operands)
        aliases = {}
        if out is not None:
            aliases = {len(operands): 0}
            in_specs.append(anywhere)
            operands.append(out)
        return pl.pallas_call(
            functools.partial(grad_kernel, n_expert, other, offset, feat_dev, starts),
            out_shape=jax.ShapeDtypeStruct((owned, hid, n_tensor * feat_dev), jnp.bfloat16),
            in_specs=in_specs,
            out_specs=anywhere,
            scratch_shapes=[
                pltpu.VMEM((owned // GROUPS, n_expert * ROOM, span), jnp.bfloat16),
                pltpu.VMEM((BUFFERS, hid, span), jnp.bfloat16),
                pltpu.SemaphoreType.DMA((BUFFERS,)),
            ],
            input_output_aliases=aliases,
            compiler_params=pltpu.CompilerParams(vmem_limit_bytes=24 * 2**20),
            cost_estimate=pl.CostEstimate(
                flops=2 * owned * hid * 256 * span,
                bytes_accessed=2 * owned * hid * span,
                transcendentals=0,
            ),
            name="weight_grad",
        )(*operands)

    shifted = passed_along(sent_grad, "pipe", -1)[0]
    widths = (feat_dev, CHUNKS[0] + NOTES) + CHUNKS[1:]
    whole, *firsts = small_call(
        join_kernel,
        [(TOK, width) for width in widths],
        [shifted, head_grad, expert_ids[0].T, probs[0].T],
        "join",
    )
    beside_whole = across(whole)
    rows, beside = [], []
    for first in firsts:
        if rows:
            rows[-1][1], first = lax.optimization_barrier((rows[-1][1], first))
        blocks = {0: first}
        blocks[1] = turned(first, "expert", 1)
        blocks[n_expert - 1] = turned(first, "expert", -1)
        for k in range(2, n_expert - 1):
            blocks[k] = turned(blocks[k - 1], "expert", 1)
        rows.append(blocks)
        beside.append({k: across(blocks[k]) for k in range(1, n_expert)})
    (place,) = small_call(
        functools.partial(place_kernel, owned),
        [(n_expert, owned * ROOM, TOK)],
        [rows[0][k] for k in range(n_expert)],
        "place",
    )
    out = None
    for c in range(len(CHUNKS)):
        out = grad_into(out, [rows[c][k] for k in range(n_expert)], (0,) * n_expert, 0, c)
        for t in range(1, n_tensor):
            blocks = [beside_whole[t]] + [beside[c][k][t] for k in range(1, n_expert)]
            starts = (sum(CHUNKS[:c]),) + (0,) * (n_expert - 1)
            out = grad_into(out, blocks, starts, n_tensor - t, c)
    return out[None]


def local(*arrays):
    owned, slot_count = arrays[4].shape[1:3]
    tokens = lax.axis_size("expert") * TOK
    by_tokens = tokens <= owned * slot_count
    return (local_by_tokens if by_tokens else local_by_slots)(*arrays)


def solution(mesh):
    in_specs = (
        P("pipe", "expert", "tensor"),
        P("expert", "tensor"),
        P("pipe", "expert", None),
        P("pipe", "expert", None),
        P("pipe", "expert", None, "tensor"),
    )
    out_specs = P("pipe", "expert", "tensor", None)
    return jax.shard_map(local, mesh=mesh, in_specs=in_specs, out_specs=out_specs, check_vma=False)
```

profile of v0, /device:TPU:20, one launch (start us, length us, event | category | flops | bytes accessed | tf_op | source)
XLA Modules:
  0.0 75.9 jit_solution(5108799347987256638)
XLA Ops:
  0.0 1.9 %collective-permute-start = (bf16[1,128,1792]{2,1,0:T(8,128)(2,1)}, bf16[1,128,1792]{2,1,0:T(8,128)(2,1)S(1)}, u32[]{:S(2)}, u32[]{:S(2)}) collective-permute-start(bf16[1,128,1792]{2,1,0:T(8,128)(2,1)} %param.5), channel_id=1, source_target_pairs={{8,0},{16,8},{24,16},{9,1},{17,9},{25,17},{10,2},{18,10},{26,18},{... | collective-permute-start | bytes 1376264 | tf_op jit(solution)/shard_map/ppermute | solution.py:24
  1.9 6.3 %collective-permute-done = bf16[1,128,1792]{2,1,0:T(8,128)(2,1)S(1)} collective-permute-done((bf16[1,128,1792]{2,1,0:T(8,128)(2,1)}, bf16[1,128,1792]{2,1,0:T(8,128)(2,1)S(1)}, u32[]{:S(2)}, u32[]{:S(2)}) %collective-permute-start) | collective-permute-done | bytes 458784 | tf_op jit(solution)/shard_map/ppermute | solution.py:24
  8.2 0.0 copy-start
  8.2 1.0 %copy-done = bf16[128,1792]{1,0:T(8,128)(2,1)S(1)} copy-done((bf16[128,1792]{1,0:T(8,128)(2,1)S(1)}, bf16[128,1792]{1,0:T(8,128)(2,1)}, u32[]{:S(2)}) %copy-start) | copy-done | bytes 458776
  9.2 0.0 copy-start.3
  9.2 0.7 copy-done.3
  9.9 0.0 copy-start.4
  9.9 0.7 copy-done.4
  10.6 0.8 %join.1 = (bf16[128,1792]{1,0:T(8,128)(2,1)}, bf16[128,896]{1,0:T(8,128)(2,1)S(1)}, bf16[128,1024]{1,0:T(8,128)(2,1)S(1)}) custom-call(bf16[128,1792]{1,0:T(8,128)(2,1)S(1)} %bitcast.15, bf16[128,1792]{1,0:T(8,128)(2,1)S(1)} %copy-done, s32[8,128]{1,0:T(8,128)S(1)} %bitcast.16, bf16[8,128]{1,0:T(8,128)(2,1)S(1)} %bitcast.17), custom_call_target="tpu_custom_call" | custom-call | tf_op jit(solution)/shard_map/join/pallas_call | solution.py:190
  11.4 0.0 copy-start.1
  11.4 1.6 %collective-permute-start.1 = (bf16[128,896]{1,0:T(8,128)(2,1)S(1)}, bf16[128,896]{1,0:T(8,128)(2,1)S(1)}, u32[]{:S(2)}, u32[]{:S(2)}) collective-permute-start(bf16[128,896]{1,0:T(8,128)(2,1)S(1)} %get-tuple-element.10.refs_0_), channel_id=1, source_target_pairs={{0,2},{2,4},{4,6},{6,0},{1,3},{3,5},{5,7},{7,1},{8,10},{10,12},{12... | collective-permute-start | bytes 688136 | tf_op jit(solution)/shard_map/ppermute | solution.py:201
  13.0 0.4 collective-permute-start.3
  13.5 4.2 %collective-permute-done.1.refs_1_ = bf16[128,896]{1,0:T(8,128)(2,1)S(1)} collective-permute-done((bf16[128,896]{1,0:T(8,128)(2,1)S(1)}, bf16[128,896]{1,0:T(8,128)(2,1)S(1)}, u32[]{:S(2)}, u32[]{:S(2)}) %collective-permute-start.1) | collective-permute-done | bytes 229408 | tf_op jit(solution)/shard_map/ppermute | solution.py:201
  17.7 1.6 %collective-permute-start.2 = (bf16[128,896]{1,0:T(8,128)(2,1)S(1)}, bf16[128,896]{1,0:T(8,128)(2,1)S(1)}, u32[]{:S(2)}, u32[]{:S(2)}) collective-permute-start(bf16[128,896]{1,0:T(8,128)(2,1)S(1)} %collective-permute-done.1.refs_1_), channel_id=1, source_target_pairs={{0,2},{2,4},{4,6},{6,0},{1,3},{3,5},{5,7},{7,1},{8,10},{10,12},{12... | collective-permute-start | bytes 688136 | tf_op jit(solution)/shard_map/ppermute | solution.py:201
  19.2 1.5 %collective-permute-start.11 = (bf16[128,896]{1,0:T(8,128)(2,1)S(1)}, bf16[128,896]{1,0:T(8,128)(2,1)}, u32[]{:S(2)}, u32[]{:S(2)}) collective-permute-start(bf16[128,896]{1,0:T(8,128)(2,1)S(1)} %collective-permute-done.1.refs_1_), channel_id=1, source_target_pairs={{0,1},{1,0},{2,3},{3,2},{4,5},{5,4},{6,7},{7,6},{8,9},{9,8},{10,11... | collective-permute-start | bytes 688136 | tf_op jit(solution)/shard_map/ppermute | solution.py:201
  20.7 0.5 collective-permute-start.4
  21.3 2.8 %pad.4 = bf16[16,4,32,512]{3,0,2,1:T(8,128)(2,1)} pad(bf16[16,4,17,512]{3,0,2,1:T(8,128)(2,1)} %bitcast.19, bf16[]{:T(256)} %constant.2.clone.1), padding=0_0x0_0x0_15x0_0 | pad | bytes 3211266 | tf_op jit(solution)/shard_map/jit(_pad)/pad | solution.py:207
  24.1 0.0 copy-done.1
  24.1 3.5 %copy.13 = bf16[16,128,512]{1,2,0:T(8,128)(2,1)S(1)} copy(bf16[16,128,512]{2,0,1:T(8,128)(2,1)} %bitcast.18) | data formatting | bytes 4194304 | tf_op jit(solution)/shard_map/reshape | solution.py:208
  27.6 2.2 %collective-permute-start.5 = (bf16[128,1024]{1,0:T(8,128)(2,1)}, bf16[128,1024]{1,0:T(8,128)(2,1)S(1)}, u32[]{:S(2)}, u32[]{:S(2)}) collective-permute-start(bf16[128,1024]{1,0:T(8,128)(2,1)} %copy-done.1), channel_id=1, source_target_pairs={{0,2},{2,4},{4,6},{6,0},{1,3},{3,5},{5,7},{7,1},{8,10},{10,12},{12... | collective-permute-start | bytes 786440 | tf_op jit(solution)/shard_map/ppermute | solution.py:201
  29.8 0.0 collective-permute-done.3.refs_3_
  29.8 0.0 collective-permute-start.9
  29.8 0.0 collective-permute-done.2.refs_2_
  29.8 1.6 %collective-permute-start.13 = (bf16[128,896]{1,0:T(8,128)(2,1)S(1)}, bf16[128,896]{1,0:T(8,128)(2,1)S(1)}, u32[]{:S(2)}, u32[]{:S(2)}) collective-permute-start(bf16[128,896]{1,0:T(8,128)(2,1)S(1)} %collective-permute-done.3.refs_3_), channel_id=1, source_target_pairs={{0,1},{1,0},{2,3},{3,2},{4,5},{5,4},{6,7},{7,6},{8,9},{9,8},{10,11... | collective-permute-start | bytes 688136 | tf_op jit(solution)/shard_map/ppermute | solution.py:201
  31.3 0.2 place.1.place_ref
  31.6 0.0 collective-permute-done.11.refs_1_
  31.6 0.6 collective-permute-start.12
  32.2 7.7 %weight_grad.4.refs_4_ = bf16[16,512,3584]{2,1,0:T(8,128)(2,1)} custom-call(bf16[4,512,128]{2,1,0:T(8,128)(2,1)S(1)} %place.1.place_ref, bf16[16,512,128]{2,1,0:T(8,128)(2,1)S(1)} %bitcast.11, bf16[128,896]{1,0:T(8,128)(2,1)S(1)} %get-tuple-element.10.refs_0_, bf16[128,896]{1,0:T(8,128)(2,1)S(1)} %collective-permute-done.1.refs_1_, ...), custom_call_target="tpu_custom_call" | custom-call | flops 3221225472 | bytes 12582912 | tf_op jit(solution)/shard_map/weight_grad/pallas_call | solution.py:219
  39.9 0.0 copy-start.2
  39.9 0.0 collective-permute-done.5.refs_1_
  39.9 2.0 %collective-permute-start.7 = (bf16[128,1024]{1,0:T(8,128)(2,1)S(1)}, bf16[128,1024]{1,0:T(8,128)(2,1)S(1)}, u32[]{:S(2)}, u32[]{:S(2)}) collective-permute-start(bf16[128,1024]{1,0:T(8,128)(2,1)S(1)} %collective-permute-done.5.refs_1_), channel_id=1, source_target_pairs={{0,2},{2,4},{4,6},{6,0},{1,3},{3,5},{5,7},{7,1},{8,10},{10,12},{12... | collective-permute-start | bytes 786440 | tf_op jit(solution)/shard_map/ppermute | solution.py:201
  41.9 0.6 collective-permute-done.13.refs_3_
  42.5 1.5 %collective-permute-start.6 = (bf16[128,1024]{1,0:T(8,128)(2,1)S(1)}, bf16[128,1024]{1,0:T(8,128)(2,1)S(1)}, u32[]{:S(2)}, u32[]{:S(2)}) collective-permute-start(bf16[128,1024]{1,0:T(8,128)(2,1)S(1)} %collective-permute-done.5.refs_1_), channel_id=1, source_target_pairs={{0,1},{1,0},{2,3},{3,2},{4,5},{5,4},{6,7},{7,6},{8,9},{9,8},{10,11... | collective-permute-start | bytes 786440 | tf_op jit(solution)/shard_map/ppermute | solution.py:201
  44.0 0.0 collective-permute-done.9.refs_3_
  44.0 0.5 collective-permute-start.10
  44.5 0.0 collective-permute-done.4.refs_0_
  44.5 2.9 %collective-permute-done.12.refs_2_ = bf16[128,896]{1,0:T(8,128)(2,1)S(1)} collective-permute-done((bf16[128,896]{1,0:T(8,128)(2,1)S(1)}, bf16[128,896]{1,0:T(8,128)(2,1)S(1)}, u32[]{:S(2)}, u32[]{:S(2)}) %collective-permute-start.12) | collective-permute-done | bytes 229408 | tf_op jit(solution)/shard_map/ppermute | solution.py:201
  47.4 8.6 %weight_grad.5.refs_4_ = bf16[16,512,3584]{2,1,0:T(8,128)(2,1)} custom-call(bf16[4,512,128]{2,1,0:T(8,128)(2,1)S(1)} %place.1.place_ref, bf16[16,512,128]{2,1,0:T(8,128)(2,1)S(1)} %bitcast.12, bf16[128,1792]{1,0:T(8,128)(2,1)S(1)} %collective-permute-done.4.refs_0_, ...), custom_call_target="tpu_custom_call", output_to_operand_aliasing={{}: (6, {})} | custom-call | flops 3221225472 | bytes 12582912 | tf_op jit(solution)/shard_map/weight_grad/pallas_call | solution.py:219
  56.1 0.0 collective-permute-done.7.refs_2_
  56.1 1.6 %collective-permute-start.8 = (bf16[128,1024]{1,0:T(8,128)(2,1)S(1)}, bf16[128,1024]{1,0:T(8,128)(2,1)S(1)}, u32[]{:S(2)}, u32[]{:S(2)}) collective-permute-start(bf16[128,1024]{1,0:T(8,128)(2,1)S(1)} %collective-permute-done.7.refs_2_), channel_id=1, source_target_pairs={{0,1},{1,0},{2,3},{3,2},{4,5},{5,4},{6,7},{7,6},{8,9},{9,8},{10,11... | collective-permute-start | bytes 786440 | tf_op jit(solution)/shard_map/ppermute | solution.py:201
  57.6 0.0 copy-done.2
  57.6 9.1 %weight_grad.6.refs_4_ = bf16[16,512,3584]{2,1,0:T(8,128)(2,1)} custom-call(bf16[4,512,128]{2,1,0:T(8,128)(2,1)S(1)} %place.1.place_ref, bf16[16,512,128]{2,1,0:T(8,128)(2,1)S(1)} %bitcast.13, bf16[128,1024]{1,0:T(8,128)(2,1)S(1)} %copy-done.2, bf16[128,1024]{1,0:T(8,128)(2,1)S(1)} %collective-permute-done.5.refs_1_, ...), custom_call_target="tpu_custom_call", output_to_operand_aliasing={{}: (6, {})} | custom-call | flops 4294967296 | bytes 16777216 | tf_op jit(solution)/shard_map/weight_grad/pallas_call | solution.py:219
  66.8 0.0 collective-permute-done.6.refs_1_
  66.8 0.0 collective-permute-done.10.refs_3_
  66.8 0.0 collective-permute-done.8.refs_2_
  66.8 9.1 %weight_grad.7 = bf16[16,512,3584]{2,1,0:T(8,128)(2,1)} custom-call(bf16[4,512,128]{2,1,0:T(8,128)(2,1)S(1)} %place.1.place_ref, bf16[16,512,128]{2,1,0:T(8,128)(2,1)S(1)} %bitcast.14, bf16[128,1792]{1,0:T(8,128)(2,1)S(1)} %collective-permute-done.4.refs_0_, bf16[128,1024]{1,0:T(8,128)(2,1)S(1)} %collective-permute-done.6.refs_1_, ...), custom_call_target="tpu_custom_call", output_to_operand_aliasing={{}: (6, {})} | custom-call | flops 4294967296 | bytes 16777216 | tf_op jit(solution)/shard_map/weight_grad/pallas_call | solution.py:219
Async XLA Ops:
  0.0 8.2 %collective-permute-start = (bf16[1,128,1792]{2,1,0:T(8,128)(2,1)}, bf16[1,128,1792]{2,1,0:T(8,128)(2,1)S(1)}, u32[]{:S(2)}, u32[]{:S(2)}) collective-permute-start(bf16[1,128,1792]{2,1,0:T(8,128)(2,1)} %param.5), channel_id=1, source_target_pairs={{8,0},{16,8},{24,16},{9,1},{17,9},{25,17},{10,2},{18,10},{26,18},{... | collective-permute-start | bytes 1376264 | tf_op jit(solution)/shard_map/ppermute | solution.py:24
  8.2 1.0 %copy-start = (bf16[128,1792]{1,0:T(8,128)(2,1)S(1)}, bf16[128,1792]{1,0:T(8,128)(2,1)}, u32[]{:S(2)}) copy-start(bf16[128,1792]{1,0:T(8,128)(2,1)} %head_ref.1) | copy-start | bytes 1376260
  9.2 0.7 copy-start.3
  9.9 0.7 copy-start.4
  11.4 12.7 %copy-start.1 = (bf16[128,1024]{1,0:T(8,128)(2,1)}, bf16[128,1024]{1,0:T(8,128)(2,1)S(1)}, u32[]{:S(2)}) copy-start(bf16[128,1024]{1,0:T(8,128)(2,1)S(1)} %get-tuple-element.14.refs_0_) | copy-start | bytes 786436
  11.4 6.2 %collective-permute-start.1 = (bf16[128,896]{1,0:T(8,128)(2,1)S(1)}, bf16[128,896]{1,0:T(8,128)(2,1)S(1)}, u32[]{:S(2)}, u32[]{:S(2)}) collective-permute-start(bf16[128,896]{1,0:T(8,128)(2,1)S(1)} %get-tuple-element.10.refs_0_), channel_id=1, source_target_pairs={{0,2},{2,4},{4,6},{6,0},{1,3},{3,5},{5,7},{7,1},{8,10},{10,12},{12... | collective-permute-start | bytes 688136 | tf_op jit(solution)/shard_map/ppermute | solution.py:201
  13.0 16.7 %collective-permute-start.3 = (bf16[128,896]{1,0:T(8,128)(2,1)S(1)}, bf16[128,896]{1,0:T(8,128)(2,1)S(1)}, u32[]{:S(2)}, u32[]{:S(2)}) collective-permute-start(bf16[128,896]{1,0:T(8,128)(2,1)S(1)} %get-tuple-element.10.refs_0_), channel_id=1, source_target_pairs={{0,6},{2,0},{4,2},{6,4},{1,7},{3,1},{5,3},{7,5},{8,14},{10,8},{12,... | collective-permute-start | bytes 688136 | tf_op jit(solution)/shard_map/ppermute | solution.py:201
  17.7 12.1 %collective-permute-start.2 = (bf16[128,896]{1,0:T(8,128)(2,1)S(1)}, bf16[128,896]{1,0:T(8,128)(2,1)S(1)}, u32[]{:S(2)}, u32[]{:S(2)}) collective-permute-start(bf16[128,896]{1,0:T(8,128)(2,1)S(1)} %collective-permute-done.1.refs_1_), channel_id=1, source_target_pairs={{0,2},{2,4},{4,6},{6,0},{1,3},{3,5},{5,7},{7,1},{8,10},{10,12},{12... | collective-permute-start | bytes 688136 | tf_op jit(solution)/shard_map/ppermute | solution.py:201
  19.2 12.3 %collective-permute-start.11 = (bf16[128,896]{1,0:T(8,128)(2,1)S(1)}, bf16[128,896]{1,0:T(8,128)(2,1)}, u32[]{:S(2)}, u32[]{:S(2)}) collective-permute-start(bf16[128,896]{1,0:T(8,128)(2,1)S(1)} %collective-permute-done.1.refs_1_), channel_id=1, source_target_pairs={{0,1},{1,0},{2,3},{3,2},{4,5},{5,4},{6,7},{7,6},{8,9},{9,8},{10,11... | collective-permute-start | bytes 688136 | tf_op jit(solution)/shard_map/ppermute | solution.py:201
  20.7 23.8 %collective-permute-start.4 = (bf16[128,1792]{1,0:T(8,128)(2,1)}, bf16[128,1792]{1,0:T(8,128)(2,1)S(1)}, u32[]{:S(2)}, u32[]{:S(2)}) collective-permute-start(bf16[128,1792]{1,0:T(8,128)(2,1)} %get-tuple-element.13), channel_id=1, source_target_pairs={{0,1},{1,0},{2,3},{3,2},{4,5},{5,4},{6,7},{7,6},{8,9},{9,8},{10,11... | collective-permute-start | bytes 1376264 | tf_op jit(solution)/shard_map/ppermute | solution.py:201
  27.6 12.3 %collective-permute-start.5 = (bf16[128,1024]{1,0:T(8,128)(2,1)}, bf16[128,1024]{1,0:T(8,128)(2,1)S(1)}, u32[]{:S(2)}, u32[]{:S(2)}) collective-permute-start(bf16[128,1024]{1,0:T(8,128)(2,1)} %copy-done.1), channel_id=1, source_target_pairs={{0,2},{2,4},{4,6},{6,0},{1,3},{3,5},{5,7},{7,1},{8,10},{10,12},{12... | collective-permute-start | bytes 786440 | tf_op jit(solution)/shard_map/ppermute | solution.py:201
  29.8 14.2 %collective-permute-start.9 = (bf16[128,1024]{1,0:T(8,128)(2,1)}, bf16[128,1024]{1,0:T(8,128)(2,1)S(1)}, u32[]{:S(2)}, u32[]{:S(2)}) collective-permute-start(bf16[128,1024]{1,0:T(8,128)(2,1)} %copy-done.1), channel_id=1, source_target_pairs={{0,6},{2,0},{4,2},{6,4},{1,7},{3,1},{5,3},{7,5},{8,14},{10,8},{12,... | collective-permute-start | bytes 786440 | tf_op jit(solution)/shard_map/ppermute | solution.py:201
  29.8 12.7 %collective-permute-start.13 = (bf16[128,896]{1,0:T(8,128)(2,1)S(1)}, bf16[128,896]{1,0:T(8,128)(2,1)S(1)}, u32[]{:S(2)}, u32[]{:S(2)}) collective-permute-start(bf16[128,896]{1,0:T(8,128)(2,1)S(1)} %collective-permute-done.3.refs_3_), channel_id=1, source_target_pairs={{0,1},{1,0},{2,3},{3,2},{4,5},{5,4},{6,7},{7,6},{8,9},{9,8},{10,11... | collective-permute-start | bytes 688136 | tf_op jit(solution)/shard_map/ppermute | solution.py:201
  31.6 15.9 %collective-permute-start.12 = (bf16[128,896]{1,0:T(8,128)(2,1)S(1)}, bf16[128,896]{1,0:T(8,128)(2,1)S(1)}, u32[]{:S(2)}, u32[]{:S(2)}) collective-permute-start(bf16[128,896]{1,0:T(8,128)(2,1)S(1)} %collective-permute-done.2.refs_2_), channel_id=1, source_target_pairs={{0,1},{1,0},{2,3},{3,2},{4,5},{5,4},{6,7},{7,6},{8,9},{9,8},{10,11... | collective-permute-start | bytes 688136 | tf_op jit(solution)/shard_map/ppermute | solution.py:201
  39.9 17.8 %copy-start.2 = (bf16[128,1024]{1,0:T(8,128)(2,1)S(1)}, bf16[128,1024]{1,0:T(8,128)(2,1)}, u32[]{:S(2)}) copy-start(bf16[128,1024]{1,0:T(8,128)(2,1)} %copy-done.1) | copy-start | bytes 786436
  39.9 16.2 %collective-permute-start.7 = (bf16[128,1024]{1,0:T(8,128)(2,1)S(1)}, bf16[128,1024]{1,0:T(8,128)(2,1)S(1)}, u32[]{:S(2)}, u32[]{:S(2)}) collective-permute-start(bf16[128,1024]{1,0:T(8,128)(2,1)S(1)} %collective-permute-done.5.refs_1_), channel_id=1, source_target_pairs={{0,2},{2,4},{4,6},{6,0},{1,3},{3,5},{5,7},{7,1},{8,10},{10,12},{12... | collective-permute-start | bytes 786440 | tf_op jit(solution)/shard_map/ppermute | solution.py:201
  42.5 24.3 %collective-permute-start.6 = (bf16[128,1024]{1,0:T(8,128)(2,1)S(1)}, bf16[128,1024]{1,0:T(8,128)(2,1)S(1)}, u32[]{:S(2)}, u32[]{:S(2)}) collective-permute-start(bf16[128,1024]{1,0:T(8,128)(2,1)S(1)} %collective-permute-done.5.refs_1_), channel_id=1, source_target_pairs={{0,1},{1,0},{2,3},{3,2},{4,5},{5,4},{6,7},{7,6},{8,9},{9,8},{10,11... | collective-permute-start | bytes 786440 | tf_op jit(solution)/shard_map/ppermute | solution.py:201
  44.0 22.8 %collective-permute-start.10 = (bf16[128,1024]{1,0:T(8,128)(2,1)S(1)}, bf16[128,1024]{1,0:T(8,128)(2,1)S(1)}, u32[]{:S(2)}, u32[]{:S(2)}) collective-permute-start(bf16[128,1024]{1,0:T(8,128)(2,1)S(1)} %collective-permute-done.9.refs_3_), channel_id=1, source_target_pairs={{0,1},{1,0},{2,3},{3,2},{4,5},{5,4},{6,7},{7,6},{8,9},{9,8},{10,11... | collective-permute-start | bytes 786440 | tf_op jit(solution)/shard_map/ppermute | solution.py:201
  56.1 10.7 %collective-permute-start.8 = (bf16[128,1024]{1,0:T(8,128)(2,1)S(1)}, bf16[128,1024]{1,0:T(8,128)(2,1)S(1)}, u32[]{:S(2)}, u32[]{:S(2)}) collective-permute-start(bf16[128,1024]{1,0:T(8,128)(2,1)S(1)} %collective-permute-done.7.refs_2_), channel_id=1, source_target_pairs={{0,1},{1,0},{2,3},{3,2},{4,5},{5,4},{6,7},{7,6},{8,9},{9,8},{10,11... | collective-permute-start | bytes 786440 | tf_op jit(solution)/shard_map/ppermute | solution.py:201
where the time goes:
time: 76.3 us; the launch traced here: 75.9 us
  Pallas kernels  35.6 us (47%)
  starting transfers between devices  17.5 us (23%)
  waiting for transfers between devices  14 us (18%)
  local copies, waits for them, and re-layouts  8.7 us (11%)
    pallas_call x4, Pallas kernels, grad_into(): pl.pallas_call(functools.partial(grad_kernel, n_expert, other, offset, fe...  34.6 us
    ppermute x13, starting transfers between devices, turned(): lax.ppermute(array, axis, [(i, (i + by) % peers) for i in range(peers)])  15.6 us
    ppermute x13, waiting for transfers between devices, turned(): lax.ppermute(array, axis, [(i, (i + by) % peers) for i in range(peers)])  7.71 us
    ppermute x1, waiting for transfers between devices, passed_along(): return lax.ppermute(array, axis, pairs)  6.29 us
    reshape x1, local copies, waits for them, and re-layouts, local_by_tokens(): act = jnp.swapaxes(act.reshape(owned, n_expert * ROOM, hid), 1, 2)  3.46 us
    pad x1, local copies, waits for them, and re-layouts, local_by_tokens(): act = jnp.pad(act, ((0, 0), (0, 0), (0, ROOM - MOST), (0, 0)))  2.84 us
    unnamed x10, local copies, waits for them, and re-layouts  2.39 us
    ppermute x1, starting transfers between devices, passed_along(): return lax.ppermute(array, axis, pairs)  1.91 us
  transfers between devices with their start and end apart: 14, of which 4 were waited for; matrix products, arithmetic and copies ran while one was open for 8% of the time, Pallas kernels for 34%

commit v1 on v0

--- a/solution.py
+++ b/solution.py
@@ -12,10 +12,9 @@
 TOK = 128
 MOST = 17
 ROOM = 32
-GROUPS = 2
-BUFFERS = 4
 CHUNKS = (768, 1024)
 NOTES = 128
+BUFFERS = 4
 
 
 def passed_along(array, axis, by):
@@ -83,7 +82,15 @@
     return weight_grad[None]
 
 
-def join_kernel(shifted_ref, head_ref, ids_ref, probs_ref, *out_refs):
+def notes_kernel(head_ref, ids_ref, probs_ref, kept_ref, notes_ref):
+    kept_ref[...] = head_ref[...]
+    notes_ref[: 2 * TOPK] = jnp.concatenate(
+        [ids_ref[...].astype(jnp.float32), probs_ref[...].astype(jnp.float32)], axis=0
+    ).astype(jnp.bfloat16)
+    notes_ref[2 * TOPK :] = jnp.zeros((TOK - 2 * TOPK, NOTES), jnp.bfloat16)
+
+
+def join_kernel(shifted_ref, head_ref, notes_ref, *out_refs):
     is_last = lax.axis_index("pipe") == lax.axis_size("pipe") - 1
     rows = jnp.where(is_last, head_ref[...], shifted_ref[...])
     whole_ref, *chunk_refs = out_refs
@@ -92,22 +99,47 @@
     for span, chunk_ref in zip(CHUNKS, chunk_refs):
         chunk_ref[:, :span] = rows[:, offset : offset + span]
         offset += span
-    first_ref, span = chunk_refs[0], CHUNKS[0]
-    first_ref[: 2 * TOPK, span:] = jnp.concatenate(
-        [ids_ref[...].astype(jnp.float32), probs_ref[...].astype(jnp.float32)], axis=0
-    ).astype(jnp.bfloat16)
-    first_ref[2 * TOPK :, span:] = jnp.zeros((TOK - 2 * TOPK, NOTES), jnp.bfloat16)
+    chunk_refs[0][:, CHUNKS[0] :] = notes_ref[...]
+
+
+def turn_kernel(n_expert, act_ref, turned_ref):
+    owned, slot_count, _ = act_ref.shape
+    me = lax.axis_index("expert")
+    slot = lax.broadcasted_iota(jnp.int32, (slot_count, n_expert * ROOM), 0)
+    spot = lax.broadcasted_iota(jnp.int32, (slot_count, n_expert * ROOM), 1)
+    block = jnp.zeros_like(slot)
+    for b in range(1, n_expert):
+        block += (slot >= b * MOST).astype(jnp.int32)
+    back = me - block
+    back = jnp.where(back < 0, back + n_expert, back)
+    target = back * ROOM + slot - block * MOST
+    for e in range(owned):
+        turned_ref[e] = lax.dot_general(
+            act_ref[e],
+            (spot == target + e).astype(jnp.bfloat16),
+            (((0,), (0,)), ((), ())),
+            preferred_element_type=jnp.float32,
+        ).astype(jnp.bfloat16)
 
 
 def place_kernel(owned, *refs):
     *blocks, place_ref = refs
     first = lax.axis_index("expert") * owned
+    rows = place_ref.shape[1]
     experts = (first + lax.broadcasted_iota(jnp.int32, (owned, TOK), 0)).astype(jnp.float32)
     earlier = (
         lax.broadcasted_iota(jnp.int32, (TOK, TOK), 0)
         < lax.broadcasted_iota(jnp.int32, (TOK, TOK), 1)
     ).astype(jnp.float32)
-    ranks = lax.broadcasted_iota(jnp.int32, (ROOM, TOK), 0).astype(jnp.float32)
+    row = lax.broadcasted_iota(jnp.int32, (rows, owned), 0)
+    start = lax.broadcasted_iota(jnp.int32, (rows, owned), 1) * MOST
+    spread = ((row >= start) & (row < start + MOST)).astype(jnp.float32)
+    wanted = lax.broadcasted_iota(jnp.int32, (rows, TOK), 0)
+    for e in range(1, owned):
+        wanted -= MOST * (
+            lax.broadcasted_iota(jnp.int32, (rows, TOK), 0) >= e * MOST
+        ).astype(jnp.int32)
+    wanted = wanted.astype(jnp.float32)
     for k, block in enumerate(blocks):
         meta = block[: 2 * TOPK, CHUNKS[0] :].astype(jnp.float32)
         named = jnp.zeros((owned, TOK), jnp.float32)
@@ -118,21 +150,18 @@
             gate = jnp.where(hit, meta[TOPK + c : TOPK + c + 1, :], gate)
         rank = jnp.dot(named, earlier, preferred_element_type=jnp.float32)
         rank = jnp.where(named > 0.0, rank, -1.0)
-        for e in range(owned):
-            place_ref[k, e * ROOM : (e + 1) * ROOM, :] = jnp.where(
-                ranks == rank[e : e + 1, :], gate[e : e + 1, :], 0.0
-            ).astype(jnp.bfloat16)
-
-
-def grad_kernel(n_expert, other, offset, feat_dev, starts, place_ref, act_ref, *refs):
+        rank = jnp.dot(spread, rank, preferred_element_type=jnp.float32)
+        gate = jnp.dot(spread, gate, preferred_element_type=jnp.float32)
+        place_ref[k] = jnp.where(rank == wanted, gate, 0.0).astype(jnp.bfloat16)
+
+
+def grad_kernel(n_expert, other, offset, feat_dev, starts, turn, place_ref, act_ref, *refs):
     blocks = refs[:n_expert]
     out_ref, weighted_ref, done_ref, out_sem = refs[-4:]
     owned, hid, _ = act_ref.shape
     features = done_ref.shape[2]
-    me = lax.axis_index("expert")
     side = lax.rem(lax.axis_index("tensor") + other, lax.axis_size("tensor"))
     column = pl.multiple_of(side * feat_dev + offset, 128)
-    share = owned // GROUPS
 
     def leave(e):
         slot = lax.rem(e, BUFFERS)
@@ -140,38 +169,36 @@
             done_ref.at[slot], out_ref.at[e, :, pl.ds(column, features)], out_sem.at[slot]
         )
 
-    def tiles():
-        for n in range(0, features, 256):
-            yield n, min(n + 256, features)
-
-    @pl.loop(0, GROUPS)
-    def _(g):
-        first = pl.multiple_of(g * share * ROOM, share * ROOM)
+    @pl.loop(0, features // 256)
+    def _(t):
+        wide = pl.ds(pl.multiple_of(t * 256, 256), 256)
         for k in range(n_expert):
-            block = lax.rem(me + n_expert - k, n_expert)
-            spot = pl.ds(pl.multiple_of(block * ROOM, ROOM), ROOM)
-            for low, high in tiles():
-                weighted = jnp.dot(
-                    place_ref[k, pl.ds(first, share * ROOM), :],
-                    blocks[k][:, starts[k] + low : starts[k] + high],
-                    preferred_element_type=jnp.float32,
-                ).astype(jnp.bfloat16)
-                for j in range(share):
-                    weighted_ref[j, spot, low:high] = weighted[j * ROOM : (j + 1) * ROOM]
-
-        @pl.loop(0, share)
-        def _(j):
-            e = g * share + j
+            rows = pl.ds(pl.multiple_of(starts[k] + t * 256, 256), 256)
+            weighted_ref[k, :, wide] = jnp.dot(
+                place_ref[k], blocks[k][:, rows], preferred_element_type=jnp.float32
+            ).astype(jnp.bfloat16)
+
+    @pl.loop(0, owned // turn)
+    def _(p):
+        for i in range(turn):
+            e = p * turn + i
 
             @pl.when(e >= BUFFERS)
             def _():
                 leave(e - BUFFERS).wait()
 
-            for low, high in tiles():
-                done_ref[lax.rem(e, BUFFERS), :, low:high] = jnp.dot(
-                    act_ref[e], weighted_ref[j, :, low:high], preferred_element_type=jnp.float32
+        for i in range(turn):
+            e = p * turn + i
+            window = pl.ds(pl.multiple_of(e * 16, 16), ROOM)
+            for n in range(0, features, 256):
+                right = jnp.concatenate(
+                    [weighted_ref[k, window, n : n + 256] for k in range(n_expert)], axis=0
+                )
+                done_ref[lax.rem(e, BUFFERS), :, n : n + 256] = jnp.dot(
+                    act_ref[e], right, preferred_element_type=jnp.float32
                 ).astype(jnp.bfloat16)
-            leave(e).start()
+        for i in range(turn):
+            leave(p * turn + i).start()
 
     @pl.loop(owned - BUFFERS, owned)
     def _(e):
@@ -203,11 +230,7 @@
     def across(array):
         return {t: turned(array, "tensor", t) for t in range(1, n_tensor)}
 
-    act = hidden_act[0].reshape(owned, n_expert, MOST, hid)
-    act = jnp.pad(act, ((0, 0), (0, 0), (0, ROOM - MOST), (0, 0)))
-    act = jnp.swapaxes(act.reshape(owned, n_expert * ROOM, hid), 1, 2)
-
-    def grad_into(out, blocks, starts, other, chunk):
+    def grad_into(out, blocks, starts, other, chunk, turn):
         span, offset = CHUNKS[chunk], sum(CHUNKS[:chunk])
         operands = [place, act, *blocks]
         in_specs = [vmem] * len(operands)
@@ -217,12 +240,12 @@
             in_specs.append(anywhere)
             operands.append(out)
         return pl.pallas_call(
-            functools.partial(grad_kernel, n_expert, other, offset, feat_dev, starts),
+            functools.partial(grad_kernel, n_expert, other, offset, feat_dev, starts, turn),
             out_shape=jax.ShapeDtypeStruct((owned, hid, n_tensor * feat_dev), jnp.bfloat16),
             in_specs=in_specs,
             out_specs=anywhere,
             scratch_shapes=[
-                pltpu.VMEM((owned // GROUPS, n_expert * ROOM, span), jnp.bfloat16),
+                pltpu.VMEM((n_expert, place.shape[1], span), jnp.bfloat16),
                 pltpu.VMEM((BUFFERS, hid, span), jnp.bfloat16),
                 pltpu.SemaphoreType.DMA((BUFFERS,)),
             ],
@@ -238,44 +261,55 @@
 
     shifted = passed_along(sent_grad, "pipe", -1)[0]
     widths = (feat_dev, CHUNKS[0] + NOTES) + CHUNKS[1:]
+    kept, notes = small_call(
+        notes_kernel,
+        [head_grad.shape, (TOK, NOTES)],
+        [head_grad, expert_ids[0].T, probs[0].T],
+        "notes",
+    )
+    shifted, kept, notes, act = lax.optimization_barrier((shifted, kept, notes, hidden_act[0]))
+    (act,) = small_call(
+        functools.partial(turn_kernel, n_expert), [(owned, hid, n_expert * ROOM)], [act], "turn"
+    )
     whole, *firsts = small_call(
-        join_kernel,
-        [(TOK, width) for width in widths],
-        [shifted, head_grad, expert_ids[0].T, probs[0].T],
-        "join",
+        join_kernel, [(TOK, width) for width in widths], [shifted, kept, notes], "join"
     )
     beside_whole = across(whole)
-    rows, beside = [], []
+    rows = []
     for first in firsts:
-        if rows:
-            rows[-1][1], first = lax.optimization_barrier((rows[-1][1], first))
         blocks = {0: first}
         blocks[1] = turned(first, "expert", 1)
-        blocks[n_expert - 1] = turned(first, "expert", -1)
+        if not rows:
+            blocks[1], first, act, firsts[1:] = lax.optimization_barrier(
+                (blocks[1], first, act, firsts[1:])
+            )
         for k in range(2, n_expert - 1):
             blocks[k] = turned(blocks[k - 1], "expert", 1)
+        blocks[n_expert - 1] = turned(first, "expert", -1)
         rows.append(blocks)
-        beside.append({k: across(blocks[k]) for k in range(1, n_expert)})
+    beside = [{k: across(blocks[k]) for k in range(1, n_expert)} for blocks in rows]
     (place,) = small_call(
         functools.partial(place_kernel, owned),
-        [(n_expert, owned * ROOM, TOK)],
+        [(n_expert, 16 * (owned + 1), TOK)],
         [rows[0][k] for k in range(n_expert)],
         "place",
     )
+    turns = iter([1, 2, 1, 2])
     out = None
     for c in range(len(CHUNKS)):
-        out = grad_into(out, [rows[c][k] for k in range(n_expert)], (0,) * n_expert, 0, c)
+        blocks = [rows[c][k] for k in range(n_expert)]
+        out = grad_into(out, blocks, (0,) * n_expert, 0, c, next(turns))
         for t in range(1, n_tensor):
             blocks = [beside_whole[t]] + [beside[c][k][t] for k in range(1, n_expert)]
             starts = (sum(CHUNKS[:c]),) + (0,) * (n_expert - 1)
-            out = grad_into(out, blocks, starts, n_tensor - t, c)
+            out = grad_into(out, blocks, starts, n_tensor - t, c, next(turns))
     return out[None]
 
 
 def local(*arrays):
     owned, slot_count = arrays[4].shape[1:3]
     tokens = lax.axis_size("expert") * TOK
-    by_tokens = tokens <= owned * slot_count
+    by_tokens = owned <= 16 and tokens <= owned * slot_count
     return (local_by_tokens if by_tokens else local_by_slots)(*arrays)
 
 

time: 76.3 us -> 77.4 us (1.014)
  the two profiles are of different devices: /device:TPU:20 before, /device:TPU:1 now
where the time goes in v1:
time: 77.4 us; the launch traced here: 77.2 us
  Pallas kernels  36.2 us (47%)
  waiting for transfers between devices  20.6 us (27%)
  starting transfers between devices  15.9 us (21%)
  local copies, waits for them, and re-layouts  4.24 us (5%)
    pallas_call x4, Pallas kernels, grad_into(): pl.pallas_call(functools.partial(grad_kernel, n_expert, other, offset, fe...  34.6 us
    ppermute x13, waiting for transfers between devices, turned(): lax.ppermute(array, axis, [(i, (i + by) % peers) for i in range(peers)])  16 us
    ppermute x13, starting transfers between devices, turned(): lax.ppermute(array, axis, [(i, (i + by) % peers) for i in range(peers)])  14 us
    ppermute x1, waiting for transfers between devices, passed_along(): return lax.ppermute(array, axis, pairs)  4.64 us
    unnamed x7, local copies, waits for them, and re-layouts  4.24 us
    ppermute x1, starting transfers between devices, passed_along(): return lax.ppermute(array, axis, pairs)  1.95 us
    pallas_call x4, Pallas kernels, small_call(): pl.pallas_call(kernel, out_shape=[jax.ShapeDtypeStruct(shape, jnp.bfloat1...  1.62 us
  transfers between devices with their start and end apart: 14, of which 5 were waited for; matrix products, arithmetic and copies ran while one was open for 2% of the time, Pallas kernels for 34%

profile of v1, /device:TPU:1, one launch (start us, length us, event | category | flops | bytes accessed | tf_op | source)
XLA Modules:
  0.0 77.2 jit_solution(3041983044136469979)
XLA Ops:
  0.0 2.0 %collective-permute-start = (bf16[1,128,1792]{2,1,0:T(8,128)(2,1)}, bf16[1,128,1792]{2,1,0:T(8,128)(2,1)S(1)}, u32[]{:S(2)}, u32[]{:S(2)}) collective-permute-start(bf16[1,128,1792]{2,1,0:T(8,128)(2,1)} %param.5), channel_id=1, source_target_pairs={{8,0},{16,8},{24,16},{9,1},{17,9},{25,17},{10,2},{18,10},{26,18},{... | collective-permute-start | bytes 1376264 | tf_op jit(solution)/shard_map/ppermute | solution.py:23
  2.0 1.9 %copy.11 = bf16[1,16,68,512]{3,2,1,0:T(8,128)(2,1)S(1)} copy(bf16[1,16,68,512]{3,1,2,0:T(8,128)(2,1)} %param.9) | data formatting | bytes 2228224 | tf_op args[4]
  3.8 0.0 copy-start
  3.8 1.0 %copy-done = bf16[128,1792]{1,0:T(8,128)(2,1)S(1)} copy-done((bf16[128,1792]{1,0:T(8,128)(2,1)S(1)}, bf16[128,1792]{1,0:T(8,128)(2,1)}, u32[]{:S(2)}) %copy-start) | copy-done | bytes 458776
  4.8 0.0 copy-start.1
  4.9 0.7 copy-done.1
  5.5 0.0 copy-start.2
  5.5 0.7 copy-done.2
  6.3 4.6 %collective-permute-done = bf16[1,128,1792]{2,1,0:T(8,128)(2,1)S(1)} collective-permute-done((bf16[1,128,1792]{2,1,0:T(8,128)(2,1)}, bf16[1,128,1792]{2,1,0:T(8,128)(2,1)S(1)}, u32[]{:S(2)}, u32[]{:S(2)}) %collective-permute-start) | collective-permute-done | bytes 458784 | tf_op jit(solution)/shard_map/ppermute | solution.py:23
  10.9 0.1 join.1
  11.0 1.6 %collective-permute-start.1 = (bf16[128,896]{1,0:T(8,128)(2,1)S(1)}, bf16[128,896]{1,0:T(8,128)(2,1)S(1)}, u32[]{:S(2)}, u32[]{:S(2)}) collective-permute-start(bf16[128,896]{1,0:T(8,128)(2,1)S(1)} %get-tuple-element.27.refs_0_), channel_id=1, source_target_pairs={{0,2},{2,4},{4,6},{6,0},{1,3},{3,5},{5,7},{7,1},{8,10},{10,12},{12... | collective-permute-start | bytes 688136 | tf_op jit(solution)/shard_map/ppermute | solution.py:228
  12.6 0.8 turn.1.act_ref
  13.4 4.7 %collective-permute-done.1.refs_1_ = bf16[128,896]{1,0:T(8,128)(2,1)S(1)} collective-permute-done((bf16[128,896]{1,0:T(8,128)(2,1)S(1)}, bf16[128,896]{1,0:T(8,128)(2,1)S(1)}, u32[]{:S(2)}, u32[]{:S(2)}) %collective-permute-start.1) | collective-permute-done | bytes 229408 | tf_op jit(solution)/shard_map/ppermute | solution.py:228
  18.1 0.0 collective-permute-start.2
  18.1 3.3 %collective-permute-start.3 = (bf16[128,896]{1,0:T(8,128)(2,1)S(1)}, bf16[128,896]{1,0:T(8,128)(2,1)S(1)}, u32[]{:S(2)}, u32[]{:S(2)}) collective-permute-start(bf16[128,896]{1,0:T(8,128)(2,1)S(1)} %get-tuple-element.27.refs_0_), channel_id=1, source_target_pairs={{0,6},{2,0},{4,2},{6,4},{1,7},{3,1},{5,3},{7,5},{8,14},{10,8},{12,... | collective-permute-start | bytes 688136 | tf_op jit(solution)/shard_map/ppermute | solution.py:228
  21.4 1.2 %collective-permute-start.11 = (bf16[128,896]{1,0:T(8,128)(2,1)S(1)}, bf16[128,896]{1,0:T(8,128)(2,1)S(1)}, u32[]{:S(2)}, u32[]{:S(2)}) collective-permute-start(bf16[128,896]{1,0:T(8,128)(2,1)S(1)} %collective-permute-done.1.refs_1_), channel_id=1, source_target_pairs={{0,1},{1,0},{2,3},{3,2},{4,5},{5,4},{6,7},{7,6},{8,9},{9,8},{10,11... | collective-permute-start | bytes 688136 | tf_op jit(solution)/shard_map/ppermute | solution.py:228
  22.5 0.3 collective-permute-start.4
  22.8 0.0 collective-permute-start.5
  22.8 4.8 %collective-permute-done.2.refs_2_ = bf16[128,896]{1,0:T(8,128)(2,1)S(1)} collective-permute-done((bf16[128,896]{1,0:T(8,128)(2,1)S(1)}, bf16[128,896]{1,0:T(8,128)(2,1)S(1)}, u32[]{:S(2)}, u32[]{:S(2)}) %collective-permute-start.2) | collective-permute-done | bytes 229408 | tf_op jit(solution)/shard_map/ppermute | solution.py:228
  27.6 2.2 %collective-permute-start.9 = (bf16[128,1024]{1,0:T(8,128)(2,1)S(1)}, bf16[128,1024]{1,0:T(8,128)(2,1)S(1)}, u32[]{:S(2)}, u32[]{:S(2)}) collective-permute-start(bf16[128,1024]{1,0:T(8,128)(2,1)S(1)} %get-tuple-element.30.refs_0_), channel_id=1, source_target_pairs={{0,6},{2,0},{4,2},{6,4},{1,7},{3,1},{5,3},{7,5},{8,14},{10,8},{12,... | collective-permute-start | bytes 786440 | tf_op jit(solution)/shard_map/ppermute | solution.py:228
  29.7 2.4 %collective-permute-done.3.refs_3_ = bf16[128,896]{1,0:T(8,128)(2,1)S(1)} collective-permute-done((bf16[128,896]{1,0:T(8,128)(2,1)S(1)}, bf16[128,896]{1,0:T(8,128)(2,1)S(1)}, u32[]{:S(2)}, u32[]{:S(2)}) %collective-permute-start.3) | collective-permute-done | bytes 229408 | tf_op jit(solution)/shard_map/ppermute | solution.py:228
  32.1 0.6 collective-permute-start.12
  32.7 0.7 place.1.place_ref
  33.5 0.0 collective-permute-done.11.refs_1_
  33.5 1.0 %collective-permute-start.13 = (bf16[128,896]{1,0:T(8,128)(2,1)S(1)}, bf16[128,896]{1,0:T(8,128)(2,1)S(1)}, u32[]{:S(2)}, u32[]{:S(2)}) collective-permute-start(bf16[128,896]{1,0:T(8,128)(2,1)S(1)} %collective-permute-done.3.refs_3_), channel_id=1, source_target_pairs={{0,1},{1,0},{2,3},{3,2},{4,5},{5,4},{6,7},{7,6},{8,9},{9,8},{10,11... | collective-permute-start | bytes 688136 | tf_op jit(solution)/shard_map/ppermute | solution.py:228
  34.4 7.5 %weight_grad.4.refs_4_ = bf16[16,512,3584]{2,1,0:T(8,128)(2,1)} custom-call(bf16[4,272,128]{2,1,0:T(8,128)(2,1)S(1)} %place.1.place_ref, bf16[16,512,128]{2,1,0:T(8,128)(2,1)S(1)} %turn.1.act_ref, bf16[128,896]{1,0:T(8,128)(2,1)S(1)} %get-tuple-element.27.refs_0_, bf16[128,896]{1,0:T(8,128)(2,1)S(1)} %collective-permute-done.1.refs_1_, ...), custom_call_target="tpu_custom_call" | custom-call | flops 3221225472 | bytes 12582912 | tf_op jit(solution)/shard_map/weight_grad/pallas_call | solution.py:242
  41.9 0.0 collective-permute-done.5.refs_1_
  41.9 1.2 %collective-permute-start.7 = (bf16[128,1024]{1,0:T(8,128)(2,1)S(1)}, bf16[128,1024]{1,0:T(8,128)(2,1)S(1)}, u32[]{:S(2)}, u32[]{:S(2)}) collective-permute-start(bf16[128,1024]{1,0:T(8,128)(2,1)S(1)} %collective-permute-done.5.refs_1_), channel_id=1, source_target_pairs={{0,2},{2,4},{4,6},{6,0},{1,3},{3,5},{5,7},{7,1},{8,10},{10,12},{12... | collective-permute-start | bytes 786440 | tf_op jit(solution)/shard_map/ppermute | solution.py:228
  43.1 0.0 collective-permute-done.4.refs_0_
  43.1 1.4 %collective-permute-start.6 = (bf16[128,1024]{1,0:T(8,128)(2,1)S(1)}, bf16[128,1024]{1,0:T(8,128)(2,1)S(1)}, u32[]{:S(2)}, u32[]{:S(2)}) collective-permute-start(bf16[128,1024]{1,0:T(8,128)(2,1)S(1)} %collective-permute-done.5.refs_1_), channel_id=1, source_target_pairs={{0,1},{1,0},{2,3},{3,2},{4,5},{5,4},{6,7},{7,6},{8,9},{9,8},{10,11... | collective-permute-start | bytes 786440 | tf_op jit(solution)/shard_map/ppermute | solution.py:228
  44.5 0.0 collective-permute-done.9.refs_3_
  44.5 0.1 collective-permute-start.10
  44.6 0.0 collective-permute-done.12.refs_2_
  44.6 4.1 %collective-permute-done.13.refs_3_ = bf16[128,896]{1,0:T(8,128)(2,1)S(1)} collective-permute-done((bf16[128,896]{1,0:T(8,128)(2,1)S(1)}, bf16[128,896]{1,0:T(8,128)(2,1)S(1)}, u32[]{:S(2)}, u32[]{:S(2)}) %collective-permute-start.13) | collective-permute-done | bytes 229408 | tf_op jit(solution)/shard_map/ppermute | solution.py:228
  48.7 8.3 %weight_grad.5.refs_4_ = bf16[16,512,3584]{2,1,0:T(8,128)(2,1)} custom-call(bf16[4,272,128]{2,1,0:T(8,128)(2,1)S(1)} %place.1.place_ref, bf16[16,512,128]{2,1,0:T(8,128)(2,1)S(1)} %turn.1.act_ref, bf16[128,1792]{1,0:T(8,128)(2,1)S(1)} %collective-permute-done.4.refs_0_, ...), custom_call_target="tpu_custom_call", output_to_operand_aliasing={{}: (6, {})} | custom-call | flops 3221225472 | bytes 12582912 | tf_op jit(solution)/shard_map/weight_grad/pallas_call | solution.py:242
  57.0 0.0 collective-permute-done.7.refs_2_
  57.0 1.3 %collective-permute-start.8 = (bf16[128,1024]{1,0:T(8,128)(2,1)S(1)}, bf16[128,1024]{1,0:T(8,128)(2,1)S(1)}, u32[]{:S(2)}, u32[]{:S(2)}) collective-permute-start(bf16[128,1024]{1,0:T(8,128)(2,1)S(1)} %collective-permute-done.7.refs_2_), channel_id=1, source_target_pairs={{0,1},{1,0},{2,3},{3,2},{4,5},{5,4},{6,7},{7,6},{8,9},{9,8},{10,11... | collective-permute-start | bytes 786440 | tf_op jit(solution)/shard_map/ppermute | solution.py:228
  58.3 9.0 %weight_grad.6.refs_4_ = bf16[16,512,3584]{2,1,0:T(8,128)(2,1)} custom-call(bf16[4,272,128]{2,1,0:T(8,128)(2,1)S(1)} %place.1.place_ref, bf16[16,512,128]{2,1,0:T(8,128)(2,1)S(1)} %turn.1.act_ref, bf16[128,1024]{1,0:T(8,128)(2,1)S(1)} %get-tuple-element.30.refs_0_, ...), custom_call_target="tpu_custom_call", output_to_operand_aliasing={{}: (6, {})} | custom-call | flops 4294967296 | bytes 16777216 | tf_op jit(solution)/shard_map/weight_grad/pallas_call | solution.py:242
  67.2 0.0 collective-permute-done.10.refs_3_
  67.2 0.0 collective-permute-done.6.refs_1_
  67.3 0.0 collective-permute-done.8.refs_2_
  67.3 9.9 %weight_grad.7 = bf16[16,512,3584]{2,1,0:T(8,128)(2,1)} custom-call(bf16[4,272,128]{2,1,0:T(8,128)(2,1)S(1)} %place.1.place_ref, bf16[16,512,128]{2,1,0:T(8,128)(2,1)S(1)} %turn.1.act_ref, bf16[128,1792]{1,0:T(8,128)(2,1)S(1)} %collective-permute-done.4.refs_0_, ...), custom_call_target="tpu_custom_call", output_to_operand_aliasing={{}: (6, {})} | custom-call | flops 4294967296 | bytes 16777216 | tf_op jit(solution)/shard_map/weight_grad/pallas_call | solution.py:242
  (1 shorter events, 0.0 us)
Async XLA Ops:
  0.0 10.9 %collective-permute-start = (bf16[1,128,1792]{2,1,0:T(8,128)(2,1)}, bf16[1,128,1792]{2,1,0:T(8,128)(2,1)S(1)}, u32[]{:S(2)}, u32[]{:S(2)}) collective-permute-start(bf16[1,128,1792]{2,1,0:T(8,128)(2,1)} %param.5), channel_id=1, source_target_pairs={{8,0},{16,8},{24,16},{9,1},{17,9},{25,17},{10,2},{18,10},{26,18},{... | collective-permute-start | bytes 1376264 | tf_op jit(solution)/shard_map/ppermute | solution.py:23
  3.8 1.0 %copy-start = (bf16[128,1792]{1,0:T(8,128)(2,1)S(1)}, bf16[128,1792]{1,0:T(8,128)(2,1)}, u32[]{:S(2)}) copy-start(bf16[128,1792]{1,0:T(8,128)(2,1)} %head_ref.1) | copy-start | bytes 1376260
  4.8 0.7 copy-start.1
  5.5 0.7 copy-start.2
  11.0 7.1 %collective-permute-start.1 = (bf16[128,896]{1,0:T(8,128)(2,1)S(1)}, bf16[128,896]{1,0:T(8,128)(2,1)S(1)}, u32[]{:S(2)}, u32[]{:S(2)}) collective-permute-start(bf16[128,896]{1,0:T(8,128)(2,1)S(1)} %get-tuple-element.27.refs_0_), channel_id=1, source_target_pairs={{0,2},{2,4},{4,6},{6,0},{1,3},{3,5},{5,7},{7,1},{8,10},{10,12},{12... | collective-permute-start | bytes 688136 | tf_op jit(solution)/shard_map/ppermute | solution.py:228
  18.1 9.5 %collective-permute-start.2 = (bf16[128,896]{1,0:T(8,128)(2,1)S(1)}, bf16[128,896]{1,0:T(8,128)(2,1)S(1)}, u32[]{:S(2)}, u32[]{:S(2)}) collective-permute-start(bf16[128,896]{1,0:T(8,128)(2,1)S(1)} %collective-permute-done.1.refs_1_), channel_id=1, source_target_pairs={{0,2},{2,4},{4,6},{6,0},{1,3},{3,5},{5,7},{7,1},{8,10},{10,12},{12... | collective-permute-start | bytes 688136 | tf_op jit(solution)/shard_map/ppermute | solution.py:228
  18.1 14.0 %collective-permute-start.3 = (bf16[128,896]{1,0:T(8,128)(2,1)S(1)}, bf16[128,896]{1,0:T(8,128)(2,1)S(1)}, u32[]{:S(2)}, u32[]{:S(2)}) collective-permute-start(bf16[128,896]{1,0:T(8,128)(2,1)S(1)} %get-tuple-element.27.refs_0_), channel_id=1, source_target_pairs={{0,6},{2,0},{4,2},{6,4},{1,7},{3,1},{5,3},{7,5},{8,14},{10,8},{12,... | collective-permute-start | bytes 688136 | tf_op jit(solution)/shard_map/ppermute | solution.py:228
  21.4 12.1 %collective-permute-start.11 = (bf16[128,896]{1,0:T(8,128)(2,1)S(1)}, bf16[128,896]{1,0:T(8,128)(2,1)S(1)}, u32[]{:S(2)}, u32[]{:S(2)}) collective-permute-start(bf16[128,896]{1,0:T(8,128)(2,1)S(1)} %collective-permute-done.1.refs_1_), channel_id=1, source_target_pairs={{0,1},{1,0},{2,3},{3,2},{4,5},{5,4},{6,7},{7,6},{8,9},{9,8},{10,11... | collective-permute-start | bytes 688136 | tf_op jit(solution)/shard_map/ppermute | solution.py:228
  22.5 20.5 %collective-permute-start.4 = (bf16[128,1792]{1,0:T(8,128)(2,1)S(1)}, bf16[128,1792]{1,0:T(8,128)(2,1)S(1)}, u32[]{:S(2)}, u32[]{:S(2)}) collective-permute-start(bf16[128,1792]{1,0:T(8,128)(2,1)S(1)} %get-tuple-element.29), channel_id=1, source_target_pairs={{0,1},{1,0},{2,3},{3,2},{4,5},{5,4},{6,7},{7,6},{8,9},{9,8},{10,11... | collective-permute-start | bytes 1376264 | tf_op jit(solution)/shard_map/ppermute | solution.py:228
  22.8 19.1 %collective-permute-start.5 = (bf16[128,1024]{1,0:T(8,128)(2,1)S(1)}, bf16[128,1024]{1,0:T(8,128)(2,1)S(1)}, u32[]{:S(2)}, u32[]{:S(2)}) collective-permute-start(bf16[128,1024]{1,0:T(8,128)(2,1)S(1)} %get-tuple-element.30.refs_0_), channel_id=1, source_target_pairs={{0,2},{2,4},{4,6},{6,0},{1,3},{3,5},{5,7},{7,1},{8,10},{10,12},{12... | collective-permute-start | bytes 786440 | tf_op jit(solution)/shard_map/ppermute | solution.py:228
  27.6 16.9 %collective-permute-start.9 = (bf16[128,1024]{1,0:T(8,128)(2,1)S(1)}, bf16[128,1024]{1,0:T(8,128)(2,1)S(1)}, u32[]{:S(2)}, u32[]{:S(2)}) collective-permute-start(bf16[128,1024]{1,0:T(8,128)(2,1)S(1)} %get-tuple-element.30.refs_0_), channel_id=1, source_target_pairs={{0,6},{2,0},{4,2},{6,4},{1,7},{3,1},{5,3},{7,5},{8,14},{10,8},{12,... | collective-permute-start | bytes 786440 | tf_op jit(solution)/shard_map/ppermute | solution.py:228
  32.1 12.4 %collective-permute-start.12 = (bf16[128,896]{1,0:T(8,128)(2,1)S(1)}, bf16[128,896]{1,0:T(8,128)(2,1)S(1)}, u32[]{:S(2)}, u32[]{:S(2)}) collective-permute-start(bf16[128,896]{1,0:T(8,128)(2,1)S(1)} %collective-permute-done.2.refs_2_), channel_id=1, source_target_pairs={{0,1},{1,0},{2,3},{3,2},{4,5},{5,4},{6,7},{7,6},{8,9},{9,8},{10,11... | collective-permute-start | bytes 688136 | tf_op jit(solution)/shard_map/ppermute | solution.py:228
  33.5 15.2 %collective-permute-start.13 = (bf16[128,896]{1,0:T(8,128)(2,1)S(1)}, bf16[128,896]{1,0:T(8,128)(2,1)S(1)}, u32[]{:S(2)}, u32[]{:S(2)}) collective-permute-start(bf16[128,896]{1,0:T(8,128)(2,1)S(1)} %collective-permute-done.3.refs_3_), channel_id=1, source_target_pairs={{0,1},{1,0},{2,3},{3,2},{4,5},{5,4},{6,7},{7,6},{8,9},{9,8},{10,11... | collective-permute-start | bytes 688136 | tf_op jit(solution)/shard_map/ppermute | solution.py:228
  41.9 15.1 %collective-permute-start.7 = (bf16[128,1024]{1,0:T(8,128)(2,1)S(1)}, bf16[128,1024]{1,0:T(8,128)(2,1)S(1)}, u32[]{:S(2)}, u32[]{:S(2)}) collective-permute-start(bf16[128,1024]{1,0:T(8,128)(2,1)S(1)} %collective-permute-done.5.refs_1_), channel_id=1, source_target_pairs={{0,2},{2,4},{4,6},{6,0},{1,3},{3,5},{5,7},{7,1},{8,10},{10,12},{12... | collective-permute-start | bytes 786440 | tf_op jit(solution)/shard_map/ppermute | solution.py:228
  43.1 24.2 %collective-permute-start.6 = (bf16[128,1024]{1,0:T(8,128)(2,1)S(1)}, bf16[128,1024]{1,0:T(8,128)(2,1)S(1)}, u32[]{:S(2)}, u32[]{:S(2)}) collective-permute-start(bf16[128,1024]{1,0:T(8,128)(2,1)S(1)} %collective-permute-done.5.refs_1_), channel_id=1, source_target_pairs={{0,1},{1,0},{2,3},{3,2},{4,5},{5,4},{6,7},{7,6},{8,9},{9,8},{10,11... | collective-permute-start | bytes 786440 | tf_op jit(solution)/shard_map/ppermute | solution.py:228
  44.5 22.7 %collective-permute-start.10 = (bf16[128,1024]{1,0:T(8,128)(2,1)S(1)}, bf16[128,1024]{1,0:T(8,128)(2,1)S(1)}, u32[]{:S(2)}, u32[]{:S(2)}) collective-permute-start(bf16[128,1024]{1,0:T(8,128)(2,1)S(1)} %collective-permute-done.9.refs_3_), channel_id=1, source_target_pairs={{0,1},{1,0},{2,3},{3,2},{4,5},{5,4},{6,7},{7,6},{8,9},{9,8},{10,11... | collective-permute-start | bytes 786440 | tf_op jit(solution)/shard_map/ppermute | solution.py:228
  57.0 10.3 %collective-permute-start.8 = (bf16[128,1024]{1,0:T(8,128)(2,1)S(1)}, bf16[128,1024]{1,0:T(8,128)(2,1)S(1)}, u32[]{:S(2)}, u32[]{:S(2)}) collective-permute-start(bf16[128,1024]{1,0:T(8,128)(2,1)S(1)} %collective-permute-done.7.refs_2_), channel_id=1, source_target_pairs={{0,1},{1,0},{2,3},{3,2},{4,5},{5,4},{6,7},{7,6},{8,9},{9,8},{10,11... | collective-permute-start | bytes 786440 | tf_op jit(solution)/shard_map/ppermute | solution.py:228
